TPU v7x, 128 devices: a whole 4x4x4 slice. The times are simulated.
128 devices in a mesh: tm: 8 (over y, core), tile: 16 (over z, x).
Axes of the slice: x: 4, y: 4, z: 4, core: 2. Of those that a mesh axis runs over, the one named last changes fastest.
Arguments:
- latents: bfloat16 [48, 16, 64, 128], P('tm', 'tile'), may hold values from -6 to 6
- group_frames: int32 [8], P('tm'), may hold values from 4 to 6, as said below
- conv_in_weight: bfloat16 [3, 3, 3, 16, 512], replicated, may hold values from -0.3125 to 0.3125
- conv_weight: bfloat16 [3, 3, 3, 512, 256], replicated, may hold values from -0.0546875 to 0.0546875
- shortcut_weight: bfloat16 [512, 256], replicated, may hold values from -0.25 to 0.25
- bias_out: float32 [256], replicated, may hold values from -3 to 3
Outputs:
- decoded: bfloat16 [48, 64, 128, 256], P('tm', 'tile')
Inputs may be any that keep to these rules, and one draw needn't show every extreme that they name: `group_frames`: live frames of each group, which form the clip in group order; some group holds 6 and some holds 4 in every draw.
All inputs are finite; a program needn't handle non-finite values.
Results may differ from a plain program's by a relative error of at most 0.0051.
Values may be sent and summed in bfloat16 or wider, within the bound.
A program may use at most 64 MiB of HBM per device.

v0:
```python
import functools

import jax
import jax.numpy as jnp
import numpy as np
from jax import lax
from jax.experimental import pallas as pl
from jax.experimental.pallas import tpu as pltpu
from jax.sharding import PartitionSpec as P

MESH = pl.DeviceIdType.MESH
F32, BF16 = jnp.float32, jnp.bfloat16

FRAMES = 6
BACK = 4
LC, HID, OUT = 16, 512, 256
H, W = 64, 128
BAND = 4
WIN = BAND + 4


def in_weight_order():
    order = np.zeros((512, 27 * LC), np.float32)
    for a in range(3):
        for q in range(LC):
            for s in range(8):
                e, b = divmod(s, 3)
                order[a * 128 + q * 8 + s, ((a * 3 + b) * 3 + e) * LC + q] = 1
            order[384 + q * 8 + 7 - a, ((a * 3 + 2) * 3 + 2) * LC + q] = 1
    return order


def exchange_kernel(n_tm, n_tile, gf_ref, lat_ref, win_ref, order_ref, cw_ref,
                    own_ref, prev_ref, u_ref, wp_ref,
                    pad, s_own, s_next, r_own, r_prev, wbuf, ubuf,
                    send_sem, recv_sem, w_sem, u_sem):
    k, j = lax.axis_index("tm"), lax.axis_index("tile")
    last = n_tm - 1
    barrier = pltpu.get_barrier_semaphore()

    def greet(s, _):
        pl.semaphore_signal(barrier, inc=1, device_id={"tile": lax.rem(j + s, n_tile)}, device_id_type=MESH)
        return 0

    lax.fori_loop(1, n_tile, greet, 0)

    @pl.when(k > 0)
    def _():
        def greet_before(s, _):
            pl.semaphore_signal(
                barrier, inc=1, device_id={"tm": k - 1, "tile": lax.rem(j + s, n_tile)}, device_id_type=MESH
            )
            return 0

        lax.fori_loop(0, n_tile, greet_before, 0)

    def w_copy(c):
        return pltpu.make_async_copy(cw_ref.at[:, c], wbuf.at[c], w_sem.at[c])

    for c in range(9):
        w_copy(c).start()

    lat = lat_ref[...].astype(F32)
    pad[BACK:, 2:H + 2] = lat
    for row in (0, 1):
        pad[BACK:, row:row + 1] = lat[:, :1]
        pad[BACK:, H + 2 + row:H + 3 + row] = lat[:, H - 1:]
    start = jnp.clip(gf_ref[0] - BACK, 0, FRAMES - BACK) + BACK
    for f in range(BACK):
        pad[f] = pad[start + f]
    for i in range(n_tile):
        rows = pad[:, BAND * i:BAND * i + WIN]
        s_next[i] = rows[:BACK].reshape(BACK * WIN, W).astype(BF16)
        s_own[i] = rows[BACK:].reshape(FRAMES * WIN, W).astype(BF16)

    pl.semaphore_wait(barrier, n_tile - 1 + jnp.where(k < last, n_tile, 0))

    def own_copy(s):
        to = lax.rem(j + s, n_tile)
        return pltpu.make_async_remote_copy(
            src_ref=s_own.at[to], dst_ref=r_own.at[j], send_sem=send_sem.at[s], recv_sem=recv_sem.at[s],
            device_id={"tile": to}, device_id_type=MESH)

    def next_copy(s):
        to = lax.rem(j + s, n_tile)
        return pltpu.make_async_remote_copy(
            src_ref=s_next.at[to], dst_ref=r_prev.at[j], send_sem=send_sem.at[n_tile + s],
            recv_sem=recv_sem.at[n_tile + s], device_id={"tm": k + 1, "tile": to}, device_id_type=MESH)

    def run(first, fn):
        def body(s, _):
            fn(s)
            return 0

        lax.fori_loop(first, n_tile, body, 0)

    run(1, lambda s: own_copy(s).start())

    @pl.when(k < last)
    def _():
        run(0, lambda s: next_copy(s).start())

    r_own[j] = s_own[j]

    def u_copy(c):
        return pltpu.make_async_copy(ubuf.at[c], u_ref.at[:, c], u_sem.at[c])

    def prepare(c, _):
        w_copy(c).wait()
        for part in range(4):
            rows = pl.ds(part * 128, 128)
            g0, g1, g2 = (wbuf[c, a, rows].astype(F32) for a in range(3))
            even, odd = 0.5 * (g0 + g2), 0.5 * g1
            ubuf[c, 0, rows] = (even + odd).astype(BF16)
            ubuf[c, 1, rows] = (even - odd).astype(BF16)
        u_copy(c).start()
        return 0

    lax.fori_loop(0, 9, prepare, 0)
    wp_ref[...] = jnp.dot(order_ref[...], win_ref[...], preferred_element_type=F32).astype(BF16)

    run(1, lambda s: own_copy(s).wait_recv())
    own_ref[...] = r_own[...]

    @pl.when(k > 0)
    def _():
        run(0, lambda s: next_copy(s).wait_recv())
        prev_ref[...] = r_prev[...]

    @pl.when(k == 0)
    def _():
        prev_ref[...] = jnp.zeros_like(prev_ref)

    run(1, lambda s: own_copy(s).wait_send())

    @pl.when(k < last)
    def _():
        run(0, lambda s: next_copy(s).wait_send())

    def drain(c, _):
        u_copy(c).wait()
        return 0

    lax.fori_loop(0, 9, drain, 0)


def exchange(n_tm, n_tile, group_frames, latents, win, order, cw):
    vmem = pl.BlockSpec(memory_space=pltpu.VMEM)
    hbm = pl.BlockSpec(memory_space=pltpu.HBM)
    return pl.pallas_call(
        functools.partial(exchange_kernel, n_tm, n_tile),
        out_shape=(
            jax.ShapeDtypeStruct((LC, FRAMES * WIN, W), BF16),
            jax.ShapeDtypeStruct((LC, BACK * WIN, W), BF16),
            jax.ShapeDtypeStruct((2, 9, HID, OUT), BF16),
            jax.ShapeDtypeStruct((512, HID), BF16),
        ),
        in_specs=[pl.BlockSpec(memory_space=pltpu.SMEM), vmem, vmem, vmem, hbm],
        out_specs=(vmem, vmem, hbm, vmem),
        scratch_shapes=[
            pltpu.VMEM((BACK + FRAMES, H + 8, W), F32),
            pltpu.VMEM((n_tile, FRAMES * WIN, W), BF16),
            pltpu.VMEM((n_tile, BACK * WIN, W), BF16),
            pltpu.VMEM((LC, FRAMES * WIN, W), BF16),
            pltpu.VMEM((LC, BACK * WIN, W), BF16),
            pltpu.VMEM((9, 3, HID, OUT), BF16),
            pltpu.VMEM((9, 2, HID, OUT), BF16),
            pltpu.SemaphoreType.DMA((2 * n_tile,)),
            pltpu.SemaphoreType.DMA((2 * n_tile,)),
            pltpu.SemaphoreType.DMA((9,)),
            pltpu.SemaphoreType.DMA((9,)),
        ],
        compiler_params=pltpu.CompilerParams(
            collective_id=0, has_side_effects=True, vmem_limit_bytes=40 << 20
        ),
        name="exchange",
    )(group_frames, latents, win, order, cw)


def block_kernel(n_tile, gf_ref, own_ref, prev_ref, wp_ref, cw_ref, u_ref, short_ref, bias_ref, out_ref,
                 main, turned, hid, v, wts, y, staged, w_sem, o_sem):
    k, j = lax.axis_index("tm"), lax.axis_index("tile")
    own_len = gf_ref[0]

    def w_copy(i, e):
        src = (cw_ref.at[0], u_ref.at[0], u_ref.at[1], cw_ref.at[2])[i]
        return pltpu.make_async_copy(src.at[:, e], wts.at[e, i], w_sem.at[e, i])

    for e in range(3):
        for i in range(4):
            w_copy(i, e).start()

    slot = lax.broadcasted_iota(jnp.int32, (128, 128), 1) % 8

    def lanes(x, shift):
        shift = shift % 128
        return pltpu.roll(x, shift, 1) if shift else x

    def spread(f, planes):
        mid = planes.reshape(LC * WIN, W).T
        left = jnp.concatenate([mid[:1], mid[:-1]], 0)
        right = jnp.concatenate([mid[1:], mid[-1:]], 0)
        for r in range(9):
            t2 = lanes(right, 6 - r)
            turned[f, r] = t2.astype(BF16)
            if r < 6:
                taps = jnp.where(slot < 3, lanes(left, -r), jnp.where(slot < 6, lanes(mid, 3 - r), t2))
                main[f, r] = taps.astype(BF16)

    first = own_ref[:, 0:16].astype(F32)[:, :WIN]
    for g in range(2):
        pair = prev_ref[:, 16 * g:16 * g + 16].astype(F32)
        for h in range(2):
            spread(2 * g + h, jnp.where(k == 0, first, pair[:, h * WIN:(h + 1) * WIN]))
    for g in range(3):
        pair = own_ref[:, 16 * g:16 * g + 16].astype(F32)
        for h in range(2):
            spread(BACK + 2 * g + h, pair[:, h * WIN:(h + 1) * WIN])

    low, high = jnp.where(j == 0, 1, 0), jnp.where(j == n_tile - 1, BAND, BAND + 1)
    slot16 = slot.astype(F32).astype(BF16)

    def row_step(r, _):
        src = jnp.clip(r, low, high)
        acts = []
        for t in range(8):
            rest = jnp.where(slot == 7, turned[t, src + 1].astype(F32),
                             jnp.where(slot == 6, turned[t + 1, src + 2].astype(F32),
                                       turned[t + 2, src + 3].astype(F32))).astype(BF16)
            taps = jnp.concatenate([main[t, src], main[t + 1, src], main[t + 2, src], rest], 1)
            hidden = jnp.dot(taps, wp_ref[...], preferred_element_type=F32).astype(BF16)
            if t >= 2:
                hid[t - 2, r] = hidden
            half = hidden.astype(F32) * 0.5
            acts.append((half + half * jnp.tanh(half)).astype(BF16))
        for tau in range(3):
            d0, d1, d2, d3 = acts[2 * tau:2 * tau + 4]
            v[tau, 0, r] = d0 - d2
            v[tau, 1, r] = d1 + d2
            v[tau, 2, r] = d2 - d1
            v[tau, 3, r] = d1 - d3
        return 0

    lax.fori_loop(0, 6, row_step, 0)

    for e in range(3):
        for i in range(4):
            w_copy(i, e).wait()

    def o_copy(tau):
        frames = pl.ds(2 * tau, 2)
        return pltpu.make_async_copy(staged.at[frames], out_ref.at[frames], o_sem.at[tau])

    def pair_step(tau, _):
        def tap_step(e, _):
            m = []
            for i in range(4):
                total = None
                for b in range(3):
                    lhs = v[tau, i, b:b + BAND].reshape(BAND * W, HID)
                    part = jnp.dot(lhs, wts[e, i, b], preferred_element_type=F32)
                    total = part if total is None else total + part
                m.append(total)
            y[e, 0] = m[0] + m[1] + m[2]
            y[e, 1] = m[1] - m[2] - m[3]
            return 0

        lax.fori_loop(0, 3, tap_step, 0)
        for p in range(2):
            t = 2 * tau + p
            live = t < own_len
            for r in range(BAND):
                rows = pl.ds(r * W, W)
                y0, y2 = y[0, p, rows], y[2, p, rows]
                total = jnp.dot(hid[t, 1 + r], short_ref[...], preferred_element_type=F32) + bias_ref[...]
                total += y[1, p, rows]
                total += jnp.concatenate([y0[:1], y0[:-1]], 0)
                total += jnp.concatenate([y2[1:], y2[-1:]], 0)
                staged[t, r] = jnp.where(live, total, 0.0).astype(BF16)
        o_copy(tau).start()
        return 0

    lax.fori_loop(0, 3, pair_step, 0)
    for tau in range(3):
        o_copy(tau).wait()


def block(n_tile, group_frames, own, prev, wp, cw, u, short, bias):
    vmem = pl.BlockSpec(memory_space=pltpu.VMEM)
    hbm = pl.BlockSpec(memory_space=pltpu.HBM)
    return pl.pallas_call(
        functools.partial(block_kernel, n_tile),
        out_shape=jax.ShapeDtypeStruct((FRAMES, BAND, W, OUT), BF16),
        in_specs=[pl.BlockSpec(memory_space=pltpu.SMEM), vmem, vmem, vmem, hbm, hbm, vmem, vmem],
        out_specs=hbm,
        scratch_shapes=[
            pltpu.VMEM((BACK + FRAMES, 6, 128, 128), BF16),
            pltpu.VMEM((BACK + FRAMES, 9, 128, 128), BF16),
            pltpu.VMEM((FRAMES, 6, W, HID), BF16),
            pltpu.VMEM((3, 4, 6, W, HID), BF16),
            pltpu.VMEM((3, 4, 3, HID, OUT), BF16),
            pltpu.VMEM((3, 2, BAND * W, OUT), F32),
            pltpu.VMEM((FRAMES, BAND, W, OUT), BF16),
            pltpu.SemaphoreType.DMA((3, 4)),
            pltpu.SemaphoreType.DMA((3,)),
        ],
        compiler_params=pltpu.CompilerParams(vmem_limit_bytes=52 << 20),
        name="block",
    )(group_frames, own, prev, wp, cw, u, short, bias)


def per_device(n_tm, n_tile, latents, group_frames, conv_in_weight, conv_weight, shortcut_weight, bias_out):
    order = jnp.asarray(in_weight_order(), BF16)
    own, prev, u, wp = exchange(
        n_tm, n_tile, group_frames, latents.reshape(FRAMES, H, W), conv_in_weight.reshape(27 * LC, HID),
        order, conv_weight.reshape(3, 9, HID, OUT))
    return block(
        n_tile, group_frames, own, prev, wp, conv_weight.reshape(3, 3, 3, HID, OUT),
        u.reshape(2, 3, 3, HID, OUT), shortcut_weight, bias_out.reshape(1, OUT))


def solution(mesh):
    in_specs = (P("tm", "tile", None, None), P("tm"), P(), P(), P(), P())
    out_specs = P("tm", "tile", None, None)
    return jax.shard_map(
        functools.partial(per_device, mesh.shape["tm"], mesh.shape["tile"]),
        mesh=mesh, in_specs=in_specs, out_specs=out_specs, check_vma=False,
    )
```

profile of v0, /device:TPU:24, one launch (start us, length us, event | category | flops | bytes accessed | tf_op | source)
XLA Modules:
  0.0 49.6 jit_solution(16081005801097596754)
XLA Ops:
  0.0 0.0 copy-start.6
  0.7 0.0 copy-start
  0.7 3.0 %copy-done = bf16[3,3,3,512,256]{4,3,2,1,0:T(8,128)(2,1)S(1)} copy-done((bf16[3,3,3,512,256]{4,3,2,1,0:T(8,128)(2,1)S(1)}, bf16[3,3,3,512,256]{4,3,2,1,0:T(8,128)(2,1)}, u32[]{:S(2)}) %copy-start) | copy-done | bytes 7077912
  3.7 0.0 copy-start.2
  3.7 1.0 %copy-done.2 = bf16[512,432]{1,0:T(8,128)(2,1)S(1)} copy-done((bf16[512,432]{1,0:T(8,128)(2,1)S(1)}, bf16[512,432]{1,0:T(8,128)(2,1)}, u32[]{:S(2)}) %copy-start.2) | copy-done | bytes 442392
  4.7 0.0 copy-start.3
  4.7 1.0 %copy-done.3 = bf16[3,3,3,16,512]{4,3,2,1,0:T(8,128)(2,1)S(1)} copy-done((bf16[3,3,3,16,512]{4,3,2,1,0:T(8,128)(2,1)S(1)}, bf16[3,3,3,16,512]{4,3,2,1,0:T(8,128)(2,1)}, u32[]{:S(2)}) %copy-start.3) | copy-done | bytes 442392
  5.7 0.0 copy-start.5
  5.7 0.9 %copy-done.5 = bf16[6,1,64,128]{3,2,1,0:T(8,128)(2,1)S(1)} copy-done((bf16[6,1,64,128]{3,2,1,0:T(8,128)(2,1)S(1)}, bf16[6,1,64,128]{3,2,1,0:T(8,128)(2,1)}, u32[]{:S(2)}) %copy-start.5) | copy-done | bytes 98328
  6.6 0.0 copy-start.4
  6.6 14.4 %exchange.1 = (bf16[16,48,128]{2,1,0:T(8,128)(2,1)S(1)}, bf16[16,32,128]{2,1,0:T(8,128)(2,1)S(1)}, bf16[2,9,512,256]{3,2,1,0:T(8,128)(2,1)S(1)}, bf16[512,512]{1,0:T(8,128)(2,1)S(1)}) custom-call(s32[1]{0:T(128)S(6)} %copy.8.gf_ref, bf16[6,64,128]{2,1,0:T(8,128)(2,1)S(1)} %bitcast.8, bf16[432,512]{1,0:T(8,128)(2,1)S(1)} %bitcast.7, ...), custom_call_target="tpu_custom_call" | custom-call | tf_op jit(solution)/shard_map/exchange/pallas_call | solution.py:150
  21.1 0.0 copy-start.1
  21.1 2.1 %copy-done.1 = bf16[2,9,512,256]{3,2,1,0:T(8,128)(2,1)} copy-done((bf16[2,9,512,256]{3,2,1,0:T(8,128)(2,1)}, bf16[2,9,512,256]{3,2,1,0:T(8,128)(2,1)S(1)}, u32[]{:S(2)}) %copy-start.1) | copy-done | bytes 4718616
  23.2 0.0 copy-done.6
  23.2 0.0 copy-done.4
  23.2 26.4 %block.1 = bf16[6,4,128,256]{3,2,1,0:T(8,128)(2,1)} custom-call(s32[1]{0:T(128)S(6)} %copy.8.gf_ref, bf16[16,48,128]{2,1,0:T(8,128)(2,1)S(1)} %get-tuple-element.9.own_ref, bf16[16,32,128]{2,1,0:T(8,128)(2,1)S(1)} %get-tuple-element.10.prev_ref, bf16[512,512]{1,0:T(8,128)(2,1)S(1)} %get-tuple-element.11.wp_ref, bf16[3,3,3,512,256]{4,3,2,1,0:T(8,128)(2,1)} %cw_ref.1, ...), custom_call_target="tpu_custom_call" | custom-call | tf_op jit(solution)/shard_map/block/pallas_call | solution.py:291
Async XLA Ops:
  0.0 23.2 %copy-start.6 = (f32[256]{0:T(256)S(1)}, f32[256]{0:T(256)}, u32[]{:S(2)}) copy-start(f32[256]{0:T(256)} %param.12) | copy-start | bytes 3076
  0.7 3.0 %copy-start = (bf16[3,3,3,512,256]{4,3,2,1,0:T(8,128)(2,1)S(1)}, bf16[3,3,3,512,256]{4,3,2,1,0:T(8,128)(2,1)}, u32[]{:S(2)}) copy-start(bf16[3,3,3,512,256]{4,3,2,1,0:T(8,128)(2,1)} %cw_ref.1) | copy-start | bytes 21233668
  3.7 1.0 %copy-start.2 = (bf16[512,432]{1,0:T(8,128)(2,1)S(1)}, bf16[512,432]{1,0:T(8,128)(2,1)}, u32[]{:S(2)}) copy-start(bf16[512,432]{1,0:T(8,128)(2,1)} %constant.2.clone.order_ref) | copy-start | bytes 1327108
  4.7 1.0 %copy-start.3 = (bf16[3,3,3,16,512]{4,3,2,1,0:T(8,128)(2,1)S(1)}, bf16[3,3,3,16,512]{4,3,2,1,0:T(8,128)(2,1)}, u32[]{:S(2)}) copy-start(bf16[3,3,3,16,512]{4,3,2,1,0:T(8,128)(2,1)} %param.9) | copy-start | bytes 1327108
  5.7 0.9 %copy-start.5 = (bf16[6,1,64,128]{3,2,1,0:T(8,128)(2,1)S(1)}, bf16[6,1,64,128]{3,2,1,0:T(8,128)(2,1)}, u32[]{:S(2)}) copy-start(bf16[6,1,64,128]{3,2,1,0:T(8,128)(2,1)} %param.7) | copy-start | bytes 294916
  6.6 16.6 %copy-start.4 = (bf16[512,256]{1,0:T(8,128)(2,1)S(1)}, bf16[512,256]{1,0:T(8,128)(2,1)}, u32[]{:S(2)}) copy-start(bf16[512,256]{1,0:T(8,128)(2,1)} %short_ref.1) | copy-start | bytes 786436
  21.1 2.1 %copy-start.1 = (bf16[2,9,512,256]{3,2,1,0:T(8,128)(2,1)}, bf16[2,9,512,256]{3,2,1,0:T(8,128)(2,1)S(1)}, u32[]{:S(2)}) copy-start(bf16[2,9,512,256]{3,2,1,0:T(8,128)(2,1)S(1)} %get-tuple-element.12) | copy-start | bytes 14155780
where the time goes:
time: 49.9 us; the launch traced here: 49.6 us
  Pallas kernels  40.8 us (82%)
  local copies, waits for them, and re-layouts  8.09 us (16%)
  between operations  0.7 us (1%)
    pallas_call x1, Pallas kernels, block(): pl.pallas_call(functools.partial(block_kernel, n_tile), out_shape=jax.Sha...  26.4 us
    pallas_call x1, Pallas kernels, exchange(): pl.pallas_call(functools.partial(exchange_kernel, n_tm, n_tile), out_shap...  14.4 us
    unnamed x14, local copies, waits for them, and re-layouts  8.09 us

commit v1 on v0

v1 whole, which is shorter than its diff:
```python
import functools

import jax
import jax.numpy as jnp
import numpy as np
from jax import lax
from jax.experimental import pallas as pl
from jax.experimental.pallas import tpu as pltpu
from jax.sharding import PartitionSpec as P

MESH = pl.DeviceIdType.MESH
F32, BF16 = jnp.float32, jnp.bfloat16

FRAMES = 6
BACK = 4
LC, HID, OUT = 16, 512, 256
H, W = 64, 128
BAND = 4
WIN = BAND + 4


def in_weight_order():
    order = np.zeros((512, 27 * LC), np.float32)
    for a in range(3):
        for q in range(LC):
            for s in range(8):
                e, b = divmod(s, 3)
                order[a * 128 + q * 8 + s, ((a * 3 + b) * 3 + e) * LC + q] = 1
            order[384 + q * 8 + 7 - a, ((a * 3 + 2) * 3 + 2) * LC + q] = 1
    return order


def time_row_weights(g):
    def three(x0, x1, x2):
        even, odd = 0.5 * (x0 + x2), 0.5 * x1
        return x0, even + odd, even - odd, x2

    columns = [three(g[0][b], g[1][b], g[2][b]) for b in range(3)]
    return [three(columns[0][i], columns[1][i], columns[2][i]) for i in range(4)]


def exchange_kernel(n_tm, n_tile, gf_ref, lat_ref, win_ref, order_ref, cw_ref,
                    own_ref, prev_ref, u_ref, wp_ref,
                    lat_buf, win_buf, order_buf, pad, s_own, s_next, r_own, r_prev, wbuf,
                    send_sem, recv_sem, w_sem, in_sem):
    k, j = lax.axis_index("tm"), lax.axis_index("tile")
    last = n_tm - 1
    barrier = pltpu.get_barrier_semaphore()

    lat_copy = pltpu.make_async_copy(lat_ref, lat_buf, in_sem.at[0])
    win_copy = pltpu.make_async_copy(win_ref, win_buf, in_sem.at[1])
    order_copy = pltpu.make_async_copy(order_ref, order_buf, in_sem.at[2])
    lat_copy.start()

    def greet(s, _):
        pl.semaphore_signal(barrier, inc=1, device_id={"tile": lax.rem(j + s, n_tile)}, device_id_type=MESH)
        return 0

    lax.fori_loop(1, n_tile, greet, 0)

    @pl.when(k > 0)
    def _():
        def greet_before(s, _):
            pl.semaphore_signal(
                barrier, inc=1, device_id={"tm": k - 1, "tile": lax.rem(j + s, n_tile)}, device_id_type=MESH
            )
            return 0

        lax.fori_loop(0, n_tile, greet_before, 0)

    def w_copy(e):
        return pltpu.make_async_copy(cw_ref.at[:, :, e], wbuf.at[e], w_sem.at[e])

    win_copy.start()
    order_copy.start()
    for e in range(3):
        w_copy(e).start()

    lat_copy.wait()
    lat = lat_buf[...].astype(F32)
    pad[BACK:, 2:H + 2] = lat
    for row in (0, 1):
        pad[BACK:, row:row + 1] = lat[:, :1]
        pad[BACK:, H + 2 + row:H + 3 + row] = lat[:, H - 1:]
    start = jnp.clip(gf_ref[0] - BACK, 0, FRAMES - BACK) + BACK
    for f in range(BACK):
        pad[f] = pad[start + f]
    for i in range(n_tile):
        rows = pad[:, BAND * i:BAND * i + WIN]
        s_next[i] = rows[:BACK].reshape(BACK * WIN, W).astype(BF16)
        s_own[i] = rows[BACK:].reshape(FRAMES * WIN, W).astype(BF16)

    pl.semaphore_wait(barrier, n_tile - 1 + jnp.where(k < last, n_tile, 0))

    def own_copy(s):
        to = lax.rem(j + s, n_tile)
        return pltpu.make_async_remote_copy(
            src_ref=s_own.at[to], dst_ref=r_own.at[j], send_sem=send_sem.at[s], recv_sem=recv_sem.at[s],
            device_id={"tile": to}, device_id_type=MESH)

    def next_copy(s):
        to = lax.rem(j + s, n_tile)
        return pltpu.make_async_remote_copy(
            src_ref=s_next.at[to], dst_ref=r_prev.at[j], send_sem=send_sem.at[n_tile + s],
            recv_sem=recv_sem.at[n_tile + s], device_id={"tm": k + 1, "tile": to}, device_id_type=MESH)

    def run(first, fn):
        def body(s, _):
            fn(s)
            return 0

        lax.fori_loop(first, n_tile, body, 0)

    run(1, lambda s: own_copy(s).start())

    @pl.when(k < last)
    def _():
        run(0, lambda s: next_copy(s).start())

    r_own[j] = s_own[j]

    win_copy.wait()
    order_copy.wait()
    wp_ref[...] = jnp.dot(order_buf[...], win_buf[...], preferred_element_type=F32).astype(BF16)

    def prepare(e, _):
        w_copy(e).wait()

        def part(n, _):
            rows = pl.ds(pl.multiple_of(n * 32, 32), 32)
            g = [[wbuf[e, a, b, rows].astype(F32) for b in range(3)] for a in range(3)]
            made = time_row_weights(g)
            for i in range(4):
                for jj in range(4):
                    u_ref[e, 4 * i + jj, rows] = made[i][jj].astype(BF16)
            return 0

        lax.fori_loop(0, HID // 32, part, 0)
        return 0

    lax.fori_loop(0, 3, prepare, 0)

    run(1, lambda s: own_copy(s).wait_recv())
    own_ref[...] = r_own[...]

    @pl.when(k > 0)
    def _():
        run(0, lambda s: next_copy(s).wait_recv())
        prev_ref[...] = r_prev[...]

    @pl.when(k == 0)
    def _():
        prev_ref[...] = jnp.zeros_like(prev_ref)

    run(1, lambda s: own_copy(s).wait_send())

    @pl.when(k < last)
    def _():
        run(0, lambda s: next_copy(s).wait_send())


def in_hbm(x):
    return pltpu.with_memory_space_constraint(x, pltpu.HBM)


def in_vmem(x):
    return pltpu.with_memory_space_constraint(x, pltpu.VMEM)


def exchange(n_tm, n_tile, group_frames, latents, win, order, cw):
    vmem = pl.BlockSpec(memory_space=pltpu.VMEM)
    hbm = pl.BlockSpec(memory_space=pltpu.HBM)
    return pl.pallas_call(
        functools.partial(exchange_kernel, n_tm, n_tile),
        out_shape=(
            pltpu.VMEM((LC, FRAMES * WIN, W), BF16),
            pltpu.VMEM((LC, BACK * WIN, W), BF16),
            pltpu.VMEM((3, 16, HID, OUT), BF16),
            pltpu.VMEM((512, HID), BF16),
        ),
        in_specs=[pl.BlockSpec(memory_space=pltpu.SMEM), hbm, hbm, hbm, hbm],
        out_specs=(vmem, vmem, vmem, vmem),
        scratch_shapes=[
            pltpu.VMEM((FRAMES, H, W), BF16),
            pltpu.VMEM((27 * LC, HID), BF16),
            pltpu.VMEM((512, 27 * LC), BF16),
            pltpu.VMEM((BACK + FRAMES, H + 8, W), F32),
            pltpu.VMEM((n_tile, FRAMES * WIN, W), BF16),
            pltpu.VMEM((n_tile, BACK * WIN, W), BF16),
            pltpu.VMEM((LC, FRAMES * WIN, W), BF16),
            pltpu.VMEM((LC, BACK * WIN, W), BF16),
            pltpu.VMEM((3, 3, 3, HID, OUT), BF16),
            pltpu.SemaphoreType.DMA((2 * n_tile,)),
            pltpu.SemaphoreType.DMA((2 * n_tile,)),
            pltpu.SemaphoreType.DMA((3,)),
            pltpu.SemaphoreType.DMA((3,)),
        ],
        compiler_params=pltpu.CompilerParams(
            collective_id=0, has_side_effects=True, vmem_limit_bytes=20 << 20
        ),
        name="exchange",
    )(group_frames, in_hbm(latents), in_hbm(win), in_hbm(order), in_hbm(cw))


def block_kernel(n_tile, gf_ref, own_ref, prev_ref, wp_ref, u_ref, short_hbm, bias_hbm, out_ref,
                 main, turned, hid, act, va, vb, staged, short_ref, bias_ref, in_sem, o_sem):
    k, j = lax.axis_index("tm"), lax.axis_index("tile")
    own_len = gf_ref[0]
    short_copy = pltpu.make_async_copy(short_hbm, short_ref, in_sem.at[0])
    bias_copy = pltpu.make_async_copy(bias_hbm, bias_ref, in_sem.at[1])
    short_copy.start()
    bias_copy.start()

    slot = lax.broadcasted_iota(jnp.int32, (128, 128), 1) % 8

    def lanes(x, shift):
        shift = shift % 128
        return pltpu.roll(x, shift, 1) if shift else x

    def spread(f, planes):
        mid = planes.reshape(LC * WIN, W).T
        left = jnp.concatenate([mid[:1], mid[:-1]], 0)
        right = jnp.concatenate([mid[1:], mid[-1:]], 0)
        for r in range(9):
            t2 = lanes(right, 6 - r)
            turned[f, r] = t2.astype(BF16)
            if r < 6:
                taps = jnp.where(slot < 3, lanes(left, -r), jnp.where(slot < 6, lanes(mid, 3 - r), t2))
                main[f, r] = taps.astype(BF16)

    first = own_ref[:, 0:16].astype(F32)[:, :WIN]
    for g in range(2):
        pair = prev_ref[:, 16 * g:16 * g + 16].astype(F32)
        for h in range(2):
            spread(2 * g + h, jnp.where(k == 0, first, pair[:, h * WIN:(h + 1) * WIN]))
    for g in range(3):
        pair = own_ref[:, 16 * g:16 * g + 16].astype(F32)
        for h in range(2):
            spread(BACK + 2 * g + h, pair[:, h * WIN:(h + 1) * WIN])

    low, high = jnp.where(j == 0, 1, 0), jnp.where(j == n_tile - 1, BAND, BAND + 1)

    def row_step(r, _):
        src = jnp.clip(r, low, high)
        for t in range(8):
            rest = jnp.where(slot == 7, turned[t, src + 1].astype(F32),
                             jnp.where(slot == 6, turned[t + 1, src + 2].astype(F32),
                                       turned[t + 2, src + 3].astype(F32))).astype(BF16)
            taps = jnp.concatenate([main[t, src], main[t + 1, src], main[t + 2, src], rest], 1)
            hidden = jnp.dot(taps, wp_ref[...], preferred_element_type=F32).astype(BF16)
            if t >= 2:
                hid[t - 2, r] = hidden
            half = hidden.astype(F32) * 0.5
            act[r, t] = (half + half * jnp.tanh(half)).astype(BF16)
        return 0

    lax.fori_loop(0, 6, row_step, 0)

    def turn_part(tau, rho, to, rows):
        def four(x):
            return x[0] - x[2], x[1] + x[2], x[2] - x[1], x[1] - x[3]

        planes = [[act[2 * rho + b, 2 * tau + a, rows].astype(F32) for a in range(4)] for b in range(4)]
        in_time = [four(planes[b]) for b in range(4)]
        for i in range(4):
            for jj, made in enumerate(four([in_time[b][i] for b in range(4)])):
                to[4 * i + jj, rows] = made.astype(BF16)

    PARTS = W // 16

    def part_rows(n):
        return pl.ds(n * 16, 16)

    def tile_step(tau, rho, frm, next_tau, next_rho, to):
        total = [[None, None], [None, None]]
        done = 0
        for e in range(3):
            rows_out = []
            for i in range(4):
                m = []
                for jj in range(4):
                    m.append(jnp.dot(frm[4 * i + jj], u_ref[e, 4 * i + jj], preferred_element_type=F32))
                rows_out.append(((m[1] + m[2]) + m[0], (m[1] - m[2]) - m[3]))
                step = 4 * e + i + 1
                while done * 12 < step * PARTS and done < PARTS:
                    turn_part(next_tau, next_rho, to, part_rows(done))
                    done += 1
            for q in range(2):
                s = [x[q] for x in rows_out]
                for p, y in enumerate((s[0] + s[1] + s[2], s[1] - s[2] - s[3])):
                    if e == 0:
                        y = jnp.concatenate([y[:1], y[:-1]], 0)
                    if e == 2:
                        y = jnp.concatenate([y[1:], y[-1:]], 0)
                    total[p][q] = y if e == 0 else total[p][q] + y
        for p in range(2):
            t = 2 * tau + p
            for q in range(2):
                r = 2 * rho + q
                y = total[p][q] + jnp.dot(hid[t, 1 + r], short_ref[...], preferred_element_type=F32) + bias_ref[...]
                staged[t, r] = jnp.where(t < own_len, y, 0.0).astype(BF16)

    def o_copy(tau):
        frames = pl.ds(2 * tau, 2)
        return pltpu.make_async_copy(staged.at[frames], out_ref.at[frames], o_sem.at[tau])

    for n in range(PARTS):
        turn_part(0, 0, va, part_rows(n))
    short_copy.wait()
    bias_copy.wait()

    def pair_step(tau, _):
        tile_step(tau, 0, va, tau, 1, vb)
        tile_step(tau, 1, vb, jnp.minimum(tau + 1, 2), 0, va)
        o_copy(tau).start()
        return 0

    lax.fori_loop(0, 3, pair_step, 0)
    for tau in range(3):
        o_copy(tau).wait()


def block(n_tile, group_frames, own, prev, wp, u, short, bias):
    vmem = pl.BlockSpec(memory_space=pltpu.VMEM)
    hbm = pl.BlockSpec(memory_space=pltpu.HBM)
    return pl.pallas_call(
        functools.partial(block_kernel, n_tile),
        out_shape=jax.ShapeDtypeStruct((FRAMES, BAND, W, OUT), BF16),
        in_specs=[pl.BlockSpec(memory_space=pltpu.SMEM), vmem, vmem, vmem, vmem, hbm, hbm],
        out_specs=hbm,
        scratch_shapes=[
            pltpu.VMEM((BACK + FRAMES, 6, 128, 128), BF16),
            pltpu.VMEM((BACK + FRAMES, 9, 128, 128), BF16),
            pltpu.VMEM((FRAMES, 6, W, HID), BF16),
            pltpu.VMEM((6, 8, W, HID), BF16),
            pltpu.VMEM((16, W, HID), BF16),
            pltpu.VMEM((16, W, HID), BF16),
            pltpu.VMEM((FRAMES, BAND, W, OUT), BF16),
            pltpu.VMEM((HID, OUT), BF16),
            pltpu.VMEM((1, OUT), F32),
            pltpu.SemaphoreType.DMA((2,)),
            pltpu.SemaphoreType.DMA((3,)),
        ],
        compiler_params=pltpu.CompilerParams(vmem_limit_bytes=44 << 20),
        name="block",
    )(group_frames, in_vmem(own), in_vmem(prev), in_vmem(wp), in_vmem(u), in_hbm(short), in_hbm(bias))


def per_device(n_tm, n_tile, latents, group_frames, conv_in_weight, conv_weight, shortcut_weight, bias_out):
    order = jnp.asarray(in_weight_order(), BF16)
    own, prev, u, wp = exchange(
        n_tm, n_tile, group_frames, latents.reshape(FRAMES, H, W), conv_in_weight.reshape(27 * LC, HID),
        order, conv_weight)
    return block(n_tile, group_frames, own, prev, wp, u, shortcut_weight, bias_out.reshape(1, OUT))


def solution(mesh):
    in_specs = (P("tm", "tile", None, None), P("tm"), P(), P(), P(), P())
    out_specs = P("tm", "tile", None, None)
    return jax.shard_map(
        functools.partial(per_device, mesh.shape["tm"], mesh.shape["tile"]),
        mesh=mesh, in_specs=in_specs, out_specs=out_specs, check_vma=False,
    )
```

time: 49.9 us -> 37.3 us (0.75)
  local copies, waits for them, and re-layouts: 8.09 us -> 0 us
  Pallas kernels: 40.8 us -> 36.6 us
    unnamed x14 -> x0, local copies, waits for them, and re-layouts: 8.09 us -> none
    pallas_call x1, Pallas kernels: 26.4 us -> 22 us  [block(): pl.pallas_call(functools.partial(block_kernel, n_tile), out_shape=jax.Sha...]
where the time goes in v1:
time: 37.3 us; the launch traced here: 37.2 us
  Pallas kernels  36.6 us (98%)
  between operations  0.66 us (2%)
    pallas_call x1, Pallas kernels, block(): pl.pallas_call(functools.partial(block_kernel, n_tile), out_shape=jax.Sha...  22 us
    pallas_call x1, Pallas kernels, exchange(): pl.pallas_call(functools.partial(exchange_kernel, n_tm, n_tile), out_shap...  14.5 us

profile of v1, /device:TPU:24, one launch (start us, length us, event | category | flops | bytes accessed | tf_op | source)
XLA Modules:
  0.0 37.2 jit_solution(13365170874596349267)
XLA Ops:
  0.7 14.5 %exchange.1 = (bf16[16,48,128]{2,1,0:T(8,128)(2,1)S(1)}, bf16[16,32,128]{2,1,0:T(8,128)(2,1)S(1)}, bf16[3,16,512,256]{3,2,1,0:T(8,128)(2,1)S(1)}, bf16[512,512]{1,0:T(8,128)(2,1)S(1)}) custom-call(s32[1]{0:T(128)S(6)} %copy.8.gf_ref, bf16[6,64,128]{2,1,0:T(8,128)(2,1)} %bitcast.4, bf16[432,512]{1,0:T(8,128)(2,1)} %bitcast.3, ...), custom_call_target="tpu_custom_call" | custom-call | tf_op jit(solution)/shard_map/exchange/pallas_call | solution.py:173
  15.2 22.0 %block.1 = bf16[6,4,128,256]{3,2,1,0:T(8,128)(2,1)} custom-call(s32[1]{0:T(128)S(6)} %copy.8.gf_ref, bf16[16,48,128]{2,1,0:T(8,128)(2,1)S(1)} %get-tuple-element.9.own_ref, bf16[16,32,128]{2,1,0:T(8,128)(2,1)S(1)} %get-tuple-element.10.prev_ref, bf16[512,512]{1,0:T(8,128)(2,1)S(1)} %get-tuple-element.11.wp_ref, ...), custom_call_target="tpu_custom_call" | custom-call | tf_op jit(solution)/shard_map/block/pallas_call | solution.py:326

commit v2 on v1

--- a/solution.py
+++ b/solution.py
@@ -52,21 +52,17 @@
     order_copy = pltpu.make_async_copy(order_ref, order_buf, in_sem.at[2])
     lat_copy.start()
 
-    def greet(s, _):
-        pl.semaphore_signal(barrier, inc=1, device_id={"tile": lax.rem(j + s, n_tile)}, device_id_type=MESH)
-        return 0
-
-    lax.fori_loop(1, n_tile, greet, 0)
+    def greet(to):
+        pl.semaphore_signal(barrier, inc=1, device_id=to, device_id_type=MESH)
+
+    peers = [lax.rem(j + s, n_tile) for s in range(n_tile)]
+    for to in peers[1:]:
+        greet({"tile": to})
 
     @pl.when(k > 0)
     def _():
-        def greet_before(s, _):
-            pl.semaphore_signal(
-                barrier, inc=1, device_id={"tm": k - 1, "tile": lax.rem(j + s, n_tile)}, device_id_type=MESH
-            )
-            return 0
-
-        lax.fori_loop(0, n_tile, greet_before, 0)
+        for to in peers:
+            greet({"tm": k - 1, "tile": to})
 
     def w_copy(e):
         return pltpu.make_async_copy(cw_ref.at[:, :, e], wbuf.at[e], w_sem.at[e])
@@ -92,30 +88,27 @@
 
     pl.semaphore_wait(barrier, n_tile - 1 + jnp.where(k < last, n_tile, 0))
 
-    def own_copy(s):
-        to = lax.rem(j + s, n_tile)
+    def own_copy(src, dst, to):
         return pltpu.make_async_remote_copy(
-            src_ref=s_own.at[to], dst_ref=r_own.at[j], send_sem=send_sem.at[s], recv_sem=recv_sem.at[s],
+            src_ref=src, dst_ref=dst, send_sem=send_sem.at[0], recv_sem=recv_sem.at[0],
             device_id={"tile": to}, device_id_type=MESH)
 
-    def next_copy(s):
-        to = lax.rem(j + s, n_tile)
+    def next_copy(src, dst, to):
         return pltpu.make_async_remote_copy(
-            src_ref=s_next.at[to], dst_ref=r_prev.at[j], send_sem=send_sem.at[n_tile + s],
-            recv_sem=recv_sem.at[n_tile + s], device_id={"tm": k + 1, "tile": to}, device_id_type=MESH)
-
-    def run(first, fn):
-        def body(s, _):
-            fn(s)
-            return 0
-
-        lax.fori_loop(first, n_tile, body, 0)
-
-    run(1, lambda s: own_copy(s).start())
+            src_ref=src, dst_ref=dst, send_sem=send_sem.at[1], recv_sem=recv_sem.at[1],
+            device_id={"tm": k + 1, "tile": to}, device_id_type=MESH)
+
+    for to in peers[1:]:
+        own_copy(s_own.at[to], r_own.at[j], to).start()
 
     @pl.when(k < last)
     def _():
-        run(0, lambda s: next_copy(s).start())
+        for to in peers:
+            next_copy(s_next.at[to], r_prev.at[j], to).start()
+
+    others = pl.ds(0, n_tile - 1)
+    all_own = own_copy(s_own.at[others], r_own.at[others], peers[1])
+    all_next = next_copy(s_next, r_prev, j)
 
     r_own[j] = s_own[j]
 
@@ -140,23 +133,23 @@
 
     lax.fori_loop(0, 3, prepare, 0)
 
-    run(1, lambda s: own_copy(s).wait_recv())
+    all_own.wait_recv()
     own_ref[...] = r_own[...]
 
     @pl.when(k > 0)
     def _():
-        run(0, lambda s: next_copy(s).wait_recv())
+        all_next.wait_recv()
         prev_ref[...] = r_prev[...]
 
     @pl.when(k == 0)
     def _():
         prev_ref[...] = jnp.zeros_like(prev_ref)
 
-    run(1, lambda s: own_copy(s).wait_send())
+    all_own.wait_send()
 
     @pl.when(k < last)
     def _():
-        run(0, lambda s: next_copy(s).wait_send())
+        all_next.wait_send()
 
 
 def in_hbm(x):
@@ -190,8 +183,8 @@
             pltpu.VMEM((LC, FRAMES * WIN, W), BF16),
             pltpu.VMEM((LC, BACK * WIN, W), BF16),
             pltpu.VMEM((3, 3, 3, HID, OUT), BF16),
-            pltpu.SemaphoreType.DMA((2 * n_tile,)),
-            pltpu.SemaphoreType.DMA((2 * n_tile,)),
+            pltpu.SemaphoreType.DMA((2,)),
+            pltpu.SemaphoreType.DMA((2,)),
             pltpu.SemaphoreType.DMA((3,)),
             pltpu.SemaphoreType.DMA((3,)),
         ],
@@ -254,9 +247,11 @@
             act[r, t] = (half + half * jnp.tanh(half)).astype(BF16)
         return 0
 
-    lax.fori_loop(0, 6, row_step, 0)
-
-    def turn_part(tau, rho, to, rows):
+    lax.fori_loop(0, 3, lambda i, c: row_step(2 * i + 1, row_step(2 * i, c)), 0)
+
+    def turn_part(tau, rho, to, n):
+        rows = pl.ds(n * 16, 16)
+
         def four(x):
             return x[0] - x[2], x[1] + x[2], x[2] - x[1], x[1] - x[3]
 
@@ -264,15 +259,15 @@
         in_time = [four(planes[b]) for b in range(4)]
         for i in range(4):
             for jj, made in enumerate(four([in_time[b][i] for b in range(4)])):
-                to[4 * i + jj, rows] = made.astype(BF16)
+                to[4 * i + jj, pl.ds(rho * W + n * 16, 16)] = made.astype(BF16)
 
     PARTS = W // 16
 
     def part_rows(n):
         return pl.ds(n * 16, 16)
 
-    def tile_step(tau, rho, frm, next_tau, next_rho, to):
-        total = [[None, None], [None, None]]
+    def tile_step(tau, frm, to):
+        total = [[[None, None], [None, None]] for _ in range(2)]
         done = 0
         for e in range(3):
             rows_out = []
@@ -282,40 +277,38 @@
                     m.append(jnp.dot(frm[4 * i + jj], u_ref[e, 4 * i + jj], preferred_element_type=F32))
                 rows_out.append(((m[1] + m[2]) + m[0], (m[1] - m[2]) - m[3]))
                 step = 4 * e + i + 1
-                while done * 12 < step * PARTS and done < PARTS:
-                    turn_part(next_tau, next_rho, to, part_rows(done))
+                while to is not None and done * 12 < step * 2 * PARTS and done < 2 * PARTS:
+                    turn_part(tau + 1, done // PARTS, to, done % PARTS)
                     done += 1
             for q in range(2):
                 s = [x[q] for x in rows_out]
-                for p, y in enumerate((s[0] + s[1] + s[2], s[1] - s[2] - s[3])):
-                    if e == 0:
-                        y = jnp.concatenate([y[:1], y[:-1]], 0)
-                    if e == 2:
-                        y = jnp.concatenate([y[1:], y[-1:]], 0)
-                    total[p][q] = y if e == 0 else total[p][q] + y
+                for p, both in enumerate((s[0] + s[1] + s[2], s[1] - s[2] - s[3])):
+                    for rho in range(2):
+                        y = both[rho * W:(rho + 1) * W]
+                        if e == 0:
+                            y = jnp.concatenate([y[:1], y[:-1]], 0)
+                        if e == 2:
+                            y = jnp.concatenate([y[1:], y[-1:]], 0)
+                        total[rho][p][q] = y if e == 0 else total[rho][p][q] + y
         for p in range(2):
             t = 2 * tau + p
-            for q in range(2):
-                r = 2 * rho + q
-                y = total[p][q] + jnp.dot(hid[t, 1 + r], short_ref[...], preferred_element_type=F32) + bias_ref[...]
-                staged[t, r] = jnp.where(t < own_len, y, 0.0).astype(BF16)
+            for rho in range(2):
+                for q in range(2):
+                    r = 2 * rho + q
+                    y = total[rho][p][q] + jnp.dot(hid[t, 1 + r], short_ref[...], preferred_element_type=F32) + bias_ref[...]
+                    staged[t, r] = jnp.where(t < own_len, y, 0.0).astype(BF16)
 
     def o_copy(tau):
         frames = pl.ds(2 * tau, 2)
         return pltpu.make_async_copy(staged.at[frames], out_ref.at[frames], o_sem.at[tau])
 
-    for n in range(PARTS):
-        turn_part(0, 0, va, part_rows(n))
+    for n in range(2 * PARTS):
+        turn_part(0, n // PARTS, va, n % PARTS)
     short_copy.wait()
     bias_copy.wait()
-
-    def pair_step(tau, _):
-        tile_step(tau, 0, va, tau, 1, vb)
-        tile_step(tau, 1, vb, jnp.minimum(tau + 1, 2), 0, va)
+    for tau in range(3):
+        tile_step(tau, (va, vb)[tau % 2], (vb, va, None)[tau])
         o_copy(tau).start()
-        return 0
-
-    lax.fori_loop(0, 3, pair_step, 0)
     for tau in range(3):
         o_copy(tau).wait()
 
@@ -333,15 +326,15 @@
             pltpu.VMEM((BACK + FRAMES, 9, 128, 128), BF16),
             pltpu.VMEM((FRAMES, 6, W, HID), BF16),
             pltpu.VMEM((6, 8, W, HID), BF16),
-            pltpu.VMEM((16, W, HID), BF16),
-            pltpu.VMEM((16, W, HID), BF16),
+            pltpu.VMEM((16, 2 * W, HID), BF16),
+            pltpu.VMEM((16, 2 * W, HID), BF16),
             pltpu.VMEM((FRAMES, BAND, W, OUT), BF16),
             pltpu.VMEM((HID, OUT), BF16),
             pltpu.VMEM((1, OUT), F32),
             pltpu.SemaphoreType.DMA((2,)),
             pltpu.SemaphoreType.DMA((3,)),
         ],
-        compiler_params=pltpu.CompilerParams(vmem_limit_bytes=44 << 20),
+        compiler_params=pltpu.CompilerParams(vmem_limit_bytes=50 << 20),
         name="block",
     )(group_frames, in_vmem(own), in_vmem(prev), in_vmem(wp), in_vmem(u), in_hbm(short), in_hbm(bias))
 

time: 37.3 us -> 35.5 us (0.952)
  Pallas kernels: 36.6 us -> 34.6 us
    pallas_call x1, Pallas kernels: 22 us -> 20.9 us  [block(): pl.pallas_call(functools.partial(block_kernel, n_tile), out_shape=jax.Sha...]
    pallas_call x1, Pallas kernels: 14.5 us -> 13.7 us  [exchange(): pl.pallas_call(functools.partial(exchange_kernel, n_tm, n_tile), out_shap...]
where the time goes in v2:
time: 35.5 us; the launch traced here: 35.4 us
  Pallas kernels  34.6 us (97%)
  between operations  0.82 us (2%)
    pallas_call x1, Pallas kernels, block(): pl.pallas_call(functools.partial(block_kernel, n_tile), out_shape=jax.Sha...  20.9 us
    pallas_call x1, Pallas kernels, exchange(): pl.pallas_call(functools.partial(exchange_kernel, n_tm, n_tile), out_shap...  13.7 us

profile of v2, /device:TPU:24, one launch (start us, length us, event | category | flops | bytes accessed | tf_op | source)
XLA Modules:
  0.0 35.4 jit_solution(15073363399559097518)
XLA Ops:
  0.7 13.7 %exchange.1 = (bf16[16,48,128]{2,1,0:T(8,128)(2,1)S(1)}, bf16[16,32,128]{2,1,0:T(8,128)(2,1)S(1)}, bf16[3,16,512,256]{3,2,1,0:T(8,128)(2,1)S(1)}, bf16[512,512]{1,0:T(8,128)(2,1)S(1)}) custom-call(s32[1]{0:T(128)S(6)} %copy.8.gf_ref, bf16[6,64,128]{2,1,0:T(8,128)(2,1)} %bitcast.4, bf16[432,512]{1,0:T(8,128)(2,1)} %bitcast.3, ...), custom_call_target="tpu_custom_call" | custom-call | tf_op jit(solution)/shard_map/exchange/pallas_call | solution.py:166
  14.4 20.9 %block.1 = bf16[6,4,128,256]{3,2,1,0:T(8,128)(2,1)} custom-call(s32[1]{0:T(128)S(6)} %copy.8.gf_ref, bf16[16,48,128]{2,1,0:T(8,128)(2,1)S(1)} %get-tuple-element.9.own_ref, bf16[16,32,128]{2,1,0:T(8,128)(2,1)S(1)} %get-tuple-element.10.prev_ref, bf16[512,512]{1,0:T(8,128)(2,1)S(1)} %get-tuple-element.11.wp_ref, ...), custom_call_target="tpu_custom_call" | custom-call | tf_op jit(solution)/shard_map/block/pallas_call | solution.py:319

commit v3 on v2

--- a/solution.py
+++ b/solution.py
@@ -26,7 +26,7 @@
             for s in range(8):
                 e, b = divmod(s, 3)
                 order[a * 128 + q * 8 + s, ((a * 3 + b) * 3 + e) * LC + q] = 1
-            order[384 + q * 8 + 7 - a, ((a * 3 + 2) * 3 + 2) * LC + q] = 1
+            order[384 + q * 8 + a, ((a * 3 + 2) * 3 + 2) * LC + q] = 1
     return order
 
 
@@ -196,7 +196,7 @@
 
 
 def block_kernel(n_tile, gf_ref, own_ref, prev_ref, wp_ref, u_ref, short_hbm, bias_hbm, out_ref,
-                 main, turned, hid, act, va, vb, staged, short_ref, bias_ref, in_sem, o_sem):
+                 main, cols, hid, act, va, vb, staged, short_ref, bias_ref, in_sem, o_sem):
     k, j = lax.axis_index("tm"), lax.axis_index("tile")
     own_len = gf_ref[0]
     short_copy = pltpu.make_async_copy(short_hbm, short_ref, in_sem.at[0])
@@ -207,47 +207,45 @@
     slot = lax.broadcasted_iota(jnp.int32, (128, 128), 1) % 8
 
     def lanes(x, shift):
-        shift = shift % 128
-        return pltpu.roll(x, shift, 1) if shift else x
-
-    def spread(f, planes):
+        if isinstance(shift, int):
+            shift = shift % 128
+            return pltpu.roll(x, shift, 1) if shift else x
+        return pltpu.roll(x, lax.rem(shift + 128, 128), 1)
+
+    def columns_first(f):
+        if f < BACK:
+            pair = prev_ref[:, 16 * (f // 2):16 * (f // 2) + 16].astype(F32)
+            first = own_ref[:, 0:16].astype(F32)[:, :WIN]
+            planes = jnp.where(k == 0, first, pair[:, f % 2 * WIN:(f % 2 + 1) * WIN])
+        else:
+            g, h = divmod(f - BACK, 2)
+            planes = own_ref[:, 16 * g:16 * g + 16].astype(F32)[:, h * WIN:(h + 1) * WIN]
         mid = planes.reshape(LC * WIN, W).T
-        left = jnp.concatenate([mid[:1], mid[:-1]], 0)
-        right = jnp.concatenate([mid[1:], mid[-1:]], 0)
-        for r in range(9):
-            t2 = lanes(right, 6 - r)
-            turned[f, r] = t2.astype(BF16)
-            if r < 6:
-                taps = jnp.where(slot < 3, lanes(left, -r), jnp.where(slot < 6, lanes(mid, 3 - r), t2))
-                main[f, r] = taps.astype(BF16)
-
-    first = own_ref[:, 0:16].astype(F32)[:, :WIN]
-    for g in range(2):
-        pair = prev_ref[:, 16 * g:16 * g + 16].astype(F32)
-        for h in range(2):
-            spread(2 * g + h, jnp.where(k == 0, first, pair[:, h * WIN:(h + 1) * WIN]))
-    for g in range(3):
-        pair = own_ref[:, 16 * g:16 * g + 16].astype(F32)
-        for h in range(2):
-            spread(BACK + 2 * g + h, pair[:, h * WIN:(h + 1) * WIN])
-
-    low, high = jnp.where(j == 0, 1, 0), jnp.where(j == n_tile - 1, BAND, BAND + 1)
-
-    def row_step(r, _):
-        src = jnp.clip(r, low, high)
-        for t in range(8):
-            rest = jnp.where(slot == 7, turned[t, src + 1].astype(F32),
-                             jnp.where(slot == 6, turned[t + 1, src + 2].astype(F32),
-                                       turned[t + 2, src + 3].astype(F32))).astype(BF16)
-            taps = jnp.concatenate([main[t, src], main[t + 1, src], main[t + 2, src], rest], 1)
-            hidden = jnp.dot(taps, wp_ref[...], preferred_element_type=F32).astype(BF16)
-            if t >= 2:
-                hid[t - 2, r] = hidden
-            half = hidden.astype(F32) * 0.5
-            act[r, t] = (half + half * jnp.tanh(half)).astype(BF16)
-        return 0
-
-    lax.fori_loop(0, 3, lambda i, c: row_step(2 * i + 1, row_step(2 * i, c)), 0)
+        cols[f, 0] = jnp.concatenate([mid[:1], mid[:-1]], 0)
+        cols[f, 1] = mid
+        cols[f, 2] = jnp.concatenate([mid[1:], mid[-1:]], 0)
+
+    source = [jnp.where(j == 0, 1, 0), 1, 2, 3, 4, jnp.where(j == n_tile - 1, BAND, BAND + 1)]
+
+    def fill(f, r):
+        at = source[r]
+        main[f, r] = jnp.where(slot < 3, lanes(cols[f, 0], -at),
+                               jnp.where(slot < 6, lanes(cols[f, 1], 3 - at), lanes(cols[f, 2], 6 - at))).astype(BF16)
+
+    def planes_of(r, ts):
+        lhs = []
+        for t in ts:
+            at = source[r] + 2
+            rest = jnp.where(slot == 0, lanes(cols[t, 2], -at),
+                             jnp.where(slot == 1, lanes(cols[t + 1, 2], 1 - at), lanes(cols[t + 2, 2], 2 - at)))
+            lhs.append(jnp.concatenate([main[t, r], main[t + 1, r], main[t + 2, r], rest.astype(BF16)], 1))
+        hidden = jnp.dot(jnp.concatenate(lhs, 0), wp_ref[...], preferred_element_type=F32).astype(BF16)
+        half = hidden.astype(F32) * 0.5
+        made = (half + half * jnp.tanh(half)).astype(BF16)
+        for n, t in enumerate(ts):
+            if t >= 2 and 1 <= r <= BAND:
+                hid[t - 2, r - 1] = hidden[n * W:(n + 1) * W]
+            act[r, t] = made[n * W:(n + 1) * W]
 
     def turn_part(tau, rho, to, n):
         rows = pl.ds(n * 16, 16)
@@ -267,19 +265,22 @@
         return pl.ds(n * 16, 16)
 
     def tile_step(tau, frm, to):
-        total = [[[None, None], [None, None]] for _ in range(2)]
-        done = 0
-        for e in range(3):
+        base = jnp.dot(hid[2 * tau:2 * tau + 2].reshape(2 * BAND * W, HID), short_ref[...], preferred_element_type=F32)
+        base = base + bias_ref[...]
+        total = [[[base[((p * 2 + rho) * 2 + q) * W:((p * 2 + rho) * 2 + q + 1) * W] for q in range(2)]
+                  for rho in range(2)] for p in range(2)]
+        done = dots = 0
+        for e in (0, 2, 1):
             rows_out = []
             for i in range(4):
                 m = []
                 for jj in range(4):
                     m.append(jnp.dot(frm[4 * i + jj], u_ref[e, 4 * i + jj], preferred_element_type=F32))
+                    dots += 1
+                    while to is not None and done * 48 < dots * 2 * PARTS:
+                        turn_part(tau + 1, done // PARTS, to, done % PARTS)
+                        done += 1
                 rows_out.append(((m[1] + m[2]) + m[0], (m[1] - m[2]) - m[3]))
-                step = 4 * e + i + 1
-                while to is not None and done * 12 < step * 2 * PARTS and done < 2 * PARTS:
-                    turn_part(tau + 1, done // PARTS, to, done % PARTS)
-                    done += 1
             for q in range(2):
                 s = [x[q] for x in rows_out]
                 for p, both in enumerate((s[0] + s[1] + s[2], s[1] - s[2] - s[3])):
@@ -289,28 +290,41 @@
                             y = jnp.concatenate([y[:1], y[:-1]], 0)
                         if e == 2:
                             y = jnp.concatenate([y[1:], y[-1:]], 0)
-                        total[rho][p][q] = y if e == 0 else total[rho][p][q] + y
+                        total[p][rho][q] = total[p][rho][q] + y
         for p in range(2):
             t = 2 * tau + p
             for rho in range(2):
                 for q in range(2):
-                    r = 2 * rho + q
-                    y = total[rho][p][q] + jnp.dot(hid[t, 1 + r], short_ref[...], preferred_element_type=F32) + bias_ref[...]
-                    staged[t, r] = jnp.where(t < own_len, y, 0.0).astype(BF16)
-
-    def o_copy(tau):
-        frames = pl.ds(2 * tau, 2)
-        return pltpu.make_async_copy(staged.at[frames], out_ref.at[frames], o_sem.at[tau])
-
-    for n in range(2 * PARTS):
-        turn_part(0, n // PARTS, va, n % PARTS)
+                    staged[t, 2 * rho + q] = jnp.where(t < own_len, total[p][rho][q], 0.0).astype(BF16)
+            o_copy(t).start()
+
+    def o_copy(t):
+        return pltpu.make_async_copy(staged.at[t], out_ref.at[t], o_sem.at[t])
+
+    for f in range(6):
+        columns_first(f)
+    for r in range(6):
+        for f in range(6):
+            fill(f, r)
+        planes_of(r, (0, 1, 2, 3))
+        if r < 4:
+            columns_first(6 + r)
+    for r in range(6):
+        fill(6, r)
+        fill(7, r)
+        planes_of(r, (4, 5))
+        for n in range(2 * PARTS * r // 6, 2 * PARTS * (r + 1) // 6):
+            turn_part(0, n // PARTS, va, n % PARTS)
+    for r in range(6):
+        fill(8, r)
+        fill(9, r)
+        planes_of(r, (6, 7))
     short_copy.wait()
     bias_copy.wait()
     for tau in range(3):
         tile_step(tau, (va, vb)[tau % 2], (vb, va, None)[tau])
-        o_copy(tau).start()
-    for tau in range(3):
-        o_copy(tau).wait()
+    for t in range(FRAMES):
+        o_copy(t).wait()
 
 
 def block(n_tile, group_frames, own, prev, wp, u, short, bias):
@@ -323,8 +337,8 @@
         out_specs=hbm,
         scratch_shapes=[
             pltpu.VMEM((BACK + FRAMES, 6, 128, 128), BF16),
-            pltpu.VMEM((BACK + FRAMES, 9, 128, 128), BF16),
-            pltpu.VMEM((FRAMES, 6, W, HID), BF16),
+            pltpu.VMEM((BACK + FRAMES, 3, 128, 128), F32),
+            pltpu.VMEM((FRAMES, BAND, W, HID), BF16),
             pltpu.VMEM((6, 8, W, HID), BF16),
             pltpu.VMEM((16, 2 * W, HID), BF16),
             pltpu.VMEM((16, 2 * W, HID), BF16),
@@ -332,7 +346,7 @@
             pltpu.VMEM((HID, OUT), BF16),
             pltpu.VMEM((1, OUT), F32),
             pltpu.SemaphoreType.DMA((2,)),
-            pltpu.SemaphoreType.DMA((3,)),
+            pltpu.SemaphoreType.DMA((FRAMES,)),
         ],
         compiler_params=pltpu.CompilerParams(vmem_limit_bytes=50 << 20),
         name="block",

time: 35.5 us -> 34.9 us (0.983)
  Pallas kernels: 34.6 us -> 34 us
    pallas_call x1, Pallas kernels: 20.9 us -> 20.2 us  [block(): pl.pallas_call(functools.partial(block_kernel, n_tile), out_shape=jax.Sha...]
where the time goes in v3:
time: 34.9 us; the launch traced here: 34.8 us
  Pallas kernels  34 us (97%)
  between operations  0.82 us (2%)
    pallas_call x1, Pallas kernels, block(): pl.pallas_call(functools.partial(block_kernel, n_tile), out_shape=jax.Sha...  20.2 us
    pallas_call x1, Pallas kernels, exchange(): pl.pallas_call(functools.partial(exchange_kernel, n_tm, n_tile), out_shap...  13.7 us

profile of v3, /device:TPU:24, one launch (start us, length us, event | category | flops | bytes accessed | tf_op | source)
XLA Modules:
  0.0 34.8 jit_solution(1643923365286608104)
XLA Ops:
  0.7 13.7 %exchange.1 = (bf16[16,48,128]{2,1,0:T(8,128)(2,1)S(1)}, bf16[16,32,128]{2,1,0:T(8,128)(2,1)S(1)}, bf16[3,16,512,256]{3,2,1,0:T(8,128)(2,1)S(1)}, bf16[512,512]{1,0:T(8,128)(2,1)S(1)}) custom-call(s32[1]{0:T(128)S(6)} %copy.8.gf_ref, bf16[6,64,128]{2,1,0:T(8,128)(2,1)} %bitcast.4, bf16[432,512]{1,0:T(8,128)(2,1)} %bitcast.3, ...), custom_call_target="tpu_custom_call" | custom-call | tf_op jit(solution)/shard_map/exchange/pallas_call | solution.py:166
  14.4 20.2 %block.1 = bf16[6,4,128,256]{3,2,1,0:T(8,128)(2,1)} custom-call(s32[1]{0:T(128)S(6)} %copy.8.gf_ref, bf16[16,48,128]{2,1,0:T(8,128)(2,1)S(1)} %get-tuple-element.9.own_ref, bf16[16,32,128]{2,1,0:T(8,128)(2,1)S(1)} %get-tuple-element.10.prev_ref, bf16[512,512]{1,0:T(8,128)(2,1)S(1)} %get-tuple-element.11.wp_ref, ...), custom_call_target="tpu_custom_call" | custom-call | tf_op jit(solution)/shard_map/block/pallas_call | solution.py:333

commit v4 on v3

--- a/solution.py
+++ b/solution.py
@@ -98,12 +98,14 @@
             src_ref=src, dst_ref=dst, send_sem=send_sem.at[1], recv_sem=recv_sem.at[1],
             device_id={"tm": k + 1, "tile": to}, device_id_type=MESH)
 
-    for to in peers[1:]:
+    for s in (10, 6, 9, 11, 14, 2, 8, 5, 7, 13, 15, 1, 3, 4, 12):
+        to = peers[s]
         own_copy(s_own.at[to], r_own.at[j], to).start()
 
     @pl.when(k < last)
     def _():
-        for to in peers:
+        for s in (10, 6, 9, 11, 14, 2, 8, 5, 7, 13, 15, 1, 3, 4, 12, 0):
+            to = peers[s]
             next_copy(s_next.at[to], r_prev.at[j], to).start()
 
     others = pl.ds(0, n_tile - 1)

time: 34.9 us -> 35.1 us (level)
  no operation moved by 1% of the time
where the time goes in v4:
time: 35.1 us; the launch traced here: 35 us
  Pallas kernels  34.2 us (97%)
  between operations  0.82 us (2%)
    pallas_call x1, Pallas kernels, block(): pl.pallas_call(functools.partial(block_kernel, n_tile), out_shape=jax.Sha...  20.2 us
    pallas_call x1, Pallas kernels, exchange(): pl.pallas_call(functools.partial(exchange_kernel, n_tm, n_tile), out_shap...  13.9 us

profile of v4, /device:TPU:24, one launch (start us, length us, event | category | flops | bytes accessed | tf_op | source)
XLA Modules:
  0.0 35.0 jit_solution(1857592437872454317)
XLA Ops:
  0.7 13.9 %exchange.1 = (bf16[16,48,128]{2,1,0:T(8,128)(2,1)S(1)}, bf16[16,32,128]{2,1,0:T(8,128)(2,1)S(1)}, bf16[3,16,512,256]{3,2,1,0:T(8,128)(2,1)S(1)}, bf16[512,512]{1,0:T(8,128)(2,1)S(1)}) custom-call(s32[1]{0:T(128)S(6)} %copy.8.gf_ref, bf16[6,64,128]{2,1,0:T(8,128)(2,1)} %bitcast.4, bf16[432,512]{1,0:T(8,128)(2,1)} %bitcast.3, ...), custom_call_target="tpu_custom_call" | custom-call | tf_op jit(solution)/shard_map/exchange/pallas_call | solution.py:168
  14.6 20.2 %block.1 = bf16[6,4,128,256]{3,2,1,0:T(8,128)(2,1)} custom-call(s32[1]{0:T(128)S(6)} %copy.8.gf_ref, bf16[16,48,128]{2,1,0:T(8,128)(2,1)S(1)} %get-tuple-element.9.own_ref, bf16[16,32,128]{2,1,0:T(8,128)(2,1)S(1)} %get-tuple-element.10.prev_ref, bf16[512,512]{1,0:T(8,128)(2,1)S(1)} %get-tuple-element.11.wp_ref, ...), custom_call_target="tpu_custom_call" | custom-call | tf_op jit(solution)/shard_map/block/pallas_call | solution.py:335
